TPU v7x, 1024 devices: a whole 4x8x16 slice. The times are simulated.
1024 devices in a mesh: ep: 32 (over z, core), tp: 4 (over x), dp: 8 (over y).
Axes of the slice: x: 4, y: 8, z: 16, core: 2. Of those that a mesh axis runs over, the one named last changes fastest.
Arguments:
- latent: bfloat16 [32768, 1024], P(('ep', 'dp')), may hold values from -6 to 6
- cotangent: bfloat16 [32768, 1024], P(('ep', 'dp')), may hold values from -6 to 6
- expert_ids: int32 [32768, 6], P(('ep', 'dp')), may hold values from 0 to 31, all different within a row; in each aligned block of 128 rows (0 to 127, 128 to 255, ...) at most 25 rows name the same one
- route_probs: float32 [32768, 6], P(('ep', 'dp')), may hold values from 0.1 to 0.4
- w_gate: bfloat16 [32, 1024, 1024], P('ep', None, 'tp'), may hold values from -0.1875 to 0.1875
- w_up: bfloat16 [32, 1024, 1024], P('ep', None, 'tp'), may hold values from -0.1875 to 0.1875
- w_down: bfloat16 [32, 1024, 1024], P('ep', 'tp'), may hold values from -0.1875 to 0.1875
Outputs:
- combined: bfloat16 [32768, 1024], P(('ep', 'dp'), 'tp')
- grad_latent: bfloat16 [32768, 1024], P(('ep', 'dp'), 'tp')
- grad_gate: float32 [32, 1024, 1024], P('ep', 'dp', 'tp')
- grad_up: float32 [32, 1024, 1024], P('ep', 'dp', 'tp')
- grad_down: float32 [32, 1024, 1024], P('ep', 'tp', 'dp')
Inputs may be any that keep to these rules, and one draw needn't show every extreme that they name: `expert_ids`: each row names 6 different experts. Among the 128 rows of one device no expert is named by more than 25 rows, and in some devices one expert is named by exactly 25.
All inputs are finite; a program needn't handle non-finite values.
Results may differ from a plain program's by a relative error of at most 0.015.
Values may be sent and summed in bfloat16 or wider, within the bound.
A program may use at most 64 MiB of HBM per device.

v0:
```python
import jax
import jax.numpy as jnp
from jax import lax
from jax.sharding import PartitionSpec as P


def local(latent, cotangent, expert_ids, route_probs, w_gate, w_up, w_down):
    tok_rows, feature_width = latent.shape
    top_count = expert_ids.shape[1]
    local_experts = w_gate.shape[0]
    sources = lax.axis_size("ep")
    experts = local_experts * sources
    capacity = max(2, tok_rows * top_count * 17 // (experts * 16))
    routes = tok_rows * top_count
    flat_ids = expert_ids.reshape(routes)
    one_hot = (flat_ids[:, None] == jnp.arange(experts, dtype=jnp.int32)[None, :]).astype(jnp.int32)
    rank_prior = jnp.cumsum(one_hot, axis=0) - one_hot
    position = jnp.sum(rank_prior * one_hot, axis=1)
    target = flat_ids * capacity + position
    route_rows = jnp.repeat(latent, top_count, axis=0)
    scaled = (
        route_probs.reshape(routes, 1)
        * jnp.repeat(cotangent, top_count, axis=0).astype(jnp.float32)
    ).astype(jnp.bfloat16)

    def pack_slots(values):
        empty = jnp.zeros((experts * capacity, values.shape[1]), jnp.bfloat16)
        return empty.at[target].set(values).reshape(experts, capacity, values.shape[1])

    inputs = lax.all_to_all(pack_slots(route_rows), "ep", split_axis=0, concat_axis=1, tiled=True)
    grads_in = lax.all_to_all(pack_slots(scaled), "ep", split_axis=0, concat_axis=1, tiled=True)
    gate_pre = jnp.einsum("erl,elf->erf", inputs, w_gate, preferred_element_type=jnp.float32)
    up_value = jnp.einsum("erl,elf->erf", inputs, w_up, preferred_element_type=jnp.float32)
    sigmoid_gate = jax.nn.sigmoid(gate_pre)
    activated = gate_pre * sigmoid_gate
    hidden = (activated * up_value).astype(jnp.bfloat16)
    out_part = jnp.einsum("erf,efl->erl", hidden, w_down, preferred_element_type=jnp.float32)
    d_hidden = jnp.einsum("erl,efl->erf", grads_in, w_down, preferred_element_type=jnp.float32)
    slope_term = sigmoid_gate * (1.0 + gate_pre * (1.0 - sigmoid_gate))
    d_gate = (d_hidden * up_value * slope_term).astype(jnp.bfloat16)
    d_up = (d_hidden * activated).astype(jnp.bfloat16)
    back_part = jnp.einsum("erf,elf->erl", d_gate, w_gate, preferred_element_type=jnp.float32)
    back_part = back_part + jnp.einsum(
        "erf,elf->erl", d_up, w_up, preferred_element_type=jnp.float32
    )
    gate_terms = jnp.einsum("erl,erf->elf", inputs, d_gate, preferred_element_type=jnp.float32)
    up_terms = jnp.einsum("erl,erf->elf", inputs, d_up, preferred_element_type=jnp.float32)
    down_terms = jnp.einsum("erf,erl->efl", hidden, grads_in, preferred_element_type=jnp.float32)
    grad_gate, grad_up, grad_down = (
        lax.psum_scatter(
            gate_terms.astype(jnp.bfloat16), "dp", scatter_dimension=1, tiled=True
        ).astype(jnp.float32),
        lax.psum_scatter(
            up_terms.astype(jnp.bfloat16), "dp", scatter_dimension=1, tiled=True
        ).astype(jnp.float32),
        lax.psum_scatter(
            down_terms.astype(jnp.bfloat16), "dp", scatter_dimension=2, tiled=True
        ).astype(jnp.float32),
    )
    summed = (
        lax.psum_scatter(
            out_part.astype(jnp.bfloat16), "tp", scatter_dimension=2, tiled=True
        ).astype(jnp.float32),
        lax.psum_scatter(
            back_part.astype(jnp.bfloat16), "tp", scatter_dimension=2, tiled=True
        ).astype(jnp.float32),
    )
    returned = (
        lax.all_to_all(
            summed[0].astype(jnp.bfloat16), "ep", split_axis=1, concat_axis=0, tiled=True
        ).astype(jnp.float32),
        lax.all_to_all(
            summed[1].astype(jnp.bfloat16), "ep", split_axis=1, concat_axis=0, tiled=True
        ).astype(jnp.float32),
    )
    slice_width = returned[0].shape[2]
    out_route = returned[0].reshape(experts * capacity, slice_width)[target]
    back_route = returned[1].reshape(experts * capacity, slice_width)[target]
    combined = jnp.sum(
        route_probs[:, :, None] * out_route.reshape(tok_rows, top_count, slice_width), axis=1
    )
    grad_latent = jnp.sum(back_route.reshape(tok_rows, top_count, slice_width), axis=1)
    return (
        combined.astype(jnp.bfloat16),
        grad_latent.astype(jnp.bfloat16),
        grad_gate,
        grad_up,
        grad_down,
    )


def solution(mesh):
    return jax.shard_map(
        local,
        mesh=mesh,
        in_specs=(
            P(("ep", "dp"), None),
            P(("ep", "dp"), None),
            P(("ep", "dp"), None),
            P(("ep", "dp"), None),
            P("ep", None, "tp"),
            P("ep", None, "tp"),
            P("ep", "tp", None),
        ),
        out_specs=(
            P(("ep", "dp"), "tp"),
            P(("ep", "dp"), "tp"),
            P("ep", "dp", "tp"),
            P("ep", "dp", "tp"),
            P("ep", "tp", "dp"),
        ),
        check_vma=False,
    )
```

profile of v0, /device:TPU:1, one launch (start us, length us, event | category | flops | bytes accessed | tf_op | source)
XLA Modules:
  0.0 485.0 jit_solution(5940223951447168362)
XLA Ops:
  11.3 2.6 broadcast_in_dim.4
  14.0 3.7 reshape.200
  17.8 6.9 %scatter_custom_fusion = bf16[800,1024]{1,0:T(8,128)(2,1)S(1)} fusion(s32[768]{0:T(1024)S(1)} %fusion.25, bf16[768,1024]{1,0:T(8,128)(2,1)} %reshape.200, bf16[]{:T(256)} %constant.6.clone.1), kind=kCustom, calls=%fused_computation.24 | custom fusion | bytes 1638912 | tf_op jit(solution)/shard_map/scatter | solution.py:28
  26.3 20.6 %all-to-all-start = ((bf16[32,25,1024]{2,1,0:T(8,128)(2,1)}), bf16[32,25,1024]{2,1,0:T(8,128)(2,1)}, u32[]{:S(2)}, u32[]{:S(2)}) async-start(bf16[32,25,1024]{2,1,0:T(8,128)(2,1)} %reshape.169), calls=%async_computation | async-start | bytes 4194304 | tf_op jit(solution)/shard_map/all_to_all | solution.py:30
  49.3 4.8 convert_element_type.101
  54.4 10.2 %scatter_custom_fusion.1 = bf16[800,1024]{1,0:T(8,128)(2,1)S(1)} fusion(s32[768]{0:T(1024)S(1)} %fusion.25, f32[768,1024]{1,0:T(8,128)} %convert_element_type.101, f32[768]{0:T(1024)S(1)} %mul.73, bf16[]{:T(256)} %constant.6.clone.1), kind=kCustom, calls=%fused_computation.7 | custom fusion | flops 1572864 | bytes 4788226 | tf_op jit(solution)/shard_map/scatter | solution.py:28
  66.1 79.4 %all-to-all-done = bf16[32,25,1024]{2,1,0:T(8,128)(2,1)} async-done(((bf16[32,25,1024]{2,1,0:T(8,128)(2,1)}), bf16[32,25,1024]{2,1,0:T(8,128)(2,1)}, u32[]{:S(2)}, u32[]{:S(2)}) %all-to-all-start) | async-done | bytes 1638432 | tf_op jit(solution)/shard_map/all_to_all | solution.py:30
  145.5 5.2 %all-to-all-start.2 = ((bf16[32,25,1024]{2,1,0:T(8,128)(2,1)}), bf16[32,25,1024]{2,1,0:T(8,128)(2,1)}, u32[]{:S(2)}, u32[]{:S(2)}) async-start(bf16[32,25,1024]{2,1,0:T(8,128)(2,1)} %reshape.175), calls=%async_computation.3 | async-start | bytes 4194304 | tf_op jit(solution)/shard_map/all_to_all | solution.py:31
  155.9 94.1 %all-to-all-done.2 = bf16[32,25,1024]{2,1,0:T(8,128)(2,1)} async-done(((bf16[32,25,1024]{2,1,0:T(8,128)(2,1)}), bf16[32,25,1024]{2,1,0:T(8,128)(2,1)}, u32[]{:S(2)}, u32[]{:S(2)}) %all-to-all-start.2) | async-done | bytes 1638432 | tf_op jit(solution)/shard_map/all_to_all | solution.py:31
  250.0 2.7 reshape.176
  252.7 3.6 multiply_convert_fusion.2
  263.4 3.0 fusion.6
  269.7 17.9 %reduce-scatter.8.cloned.1.call-done = bf16[1,800,256]{2,1,0:T(8,128)(2,1)} async-done(((bf16[1,800,1024]{2,1,0:T(8,128)(2,1)}), bf16[1,800,256]{2,1,0:T(8,128)(2,1)}) %reduce-scatter.8.cloned.1.call-update) | async-done | bytes 409616 | tf_op jit(solution)/shard_map/reduce_scatter | solution.py:61
  289.7 3.1 reduce.4
  293.8 14.6 %all-to-all-start.1 = ((bf16[32,2,3200]{2,1,0:T(2,128)(2,1)}), bf16[32,2,3200]{2,1,0:T(2,128)(2,1)S(1)}, u32[]{:S(2)}, u32[]{:S(2)}) async-start(bf16[32,2,3200]{2,1,0:T(2,128)(2,1)} %reshape.221), calls=%async_computation.2 | async-start | bytes 819200 | tf_op jit(solution)/shard_map/all_to_all | solution.py:69
  308.6 2.6 fusion.4
  311.2 16.8 %reduce-scatter.10.cloned.1.call-done = bf16[1,800,256]{2,1,0:T(8,128)(2,1)} async-done(((bf16[1,800,1024]{2,1,0:T(8,128)(2,1)}), bf16[1,800,256]{2,1,0:T(8,128)(2,1)}) %reduce-scatter.10.cloned.1.call-update) | async-done | bytes 409616 | tf_op jit(solution)/shard_map/reduce_scatter | solution.py:64
  329.7 3.9 reduce.5
  337.1 13.0 %all-to-all-start.3 = ((bf16[32,2,3200]{2,1,0:T(2,128)(2,1)}), bf16[32,2,3200]{2,1,0:T(2,128)(2,1)}, u32[]{:S(2)}, u32[]{:S(2)}) async-start(bf16[32,2,3200]{2,1,0:T(2,128)(2,1)} %reshape.223), calls=%async_computation.5 | async-start | bytes 819200 | tf_op jit(solution)/shard_map/all_to_all | solution.py:72
  350.2 2.6 fusion.5
  352.7 20.2 %reduce-scatter.16.cloned.1.call-done = bf16[128,256]{1,0:T(8,128)(2,1)} async-done(((bf16[1024,256]{1,0:T(8,128)(2,1)}), bf16[128,256]{1,0:T(8,128)(2,1)}) %reduce-scatter.16.cloned.1.call-update) | async-done | bytes 65552
  374.6 45.2 %reduce-scatter.12.cloned.1.call-done = bf16[1,128,256]{2,1,0:T(8,128)(2,1)} async-done(((bf16[1,1024,256]{2,1,0:T(8,128)(2,1)}), bf16[1,128,256]{2,1,0:T(8,128)(2,1)}) %reduce-scatter.12.cloned.1.call-update) | async-done | bytes 65552 | tf_op jit(solution)/shard_map/reduce_scatter | solution.py:50
  421.4 46.0 %reduce-scatter.14.cloned.1.call-done = bf16[1,128,256]{2,1,0:T(8,128)(2,1)} async-done(((bf16[1,1024,256]{2,1,0:T(8,128)(2,1)}), bf16[1,128,256]{2,1,0:T(8,128)(2,1)}) %reduce-scatter.14.cloned.1.call-update) | async-done | bytes 65552 | tf_op jit(solution)/shard_map/reduce_scatter | solution.py:53
  472.5 2.8 reshape.224
  (73 shorter events, 45.6 us)
Async XLA Ops:
  7.2 245.5 %copy-start = (bf16[1,256,1024]{2,1,0:T(8,128)(2,1)S(1)}, bf16[1,256,1024]{2,1,0:T(8,128)(2,1)}, u32[]{:S(2)}) copy-start(bf16[1,256,1024]{2,1,0:T(8,128)(2,1)} %param.13) | copy-start | bytes 1572868
  26.3 20.6 %copy-start.6 = (bf16[128,1024]{1,0:T(8,128)(2,1)S(1)}, bf16[128,1024]{1,0:T(8,128)(2,1)}, u32[]{:S(2)}) copy-start(bf16[128,1024]{1,0:T(8,128)(2,1)} %param.8) | copy-start | bytes 786436
  26.3 119.2 %all-to-all-start = ((bf16[32,25,1024]{2,1,0:T(8,128)(2,1)}), bf16[32,25,1024]{2,1,0:T(8,128)(2,1)}, u32[]{:S(2)}, u32[]{:S(2)}) async-start(bf16[32,25,1024]{2,1,0:T(8,128)(2,1)} %reshape.169), calls=%async_computation | async-start | bytes 4194304 | tf_op jit(solution)/shard_map/all_to_all | solution.py:30
  49.3 4.8 copy-start.7
  145.5 104.5 %all-to-all-start.2 = ((bf16[32,25,1024]{2,1,0:T(8,128)(2,1)}), bf16[32,25,1024]{2,1,0:T(8,128)(2,1)}, u32[]{:S(2)}, u32[]{:S(2)}) async-start(bf16[32,25,1024]{2,1,0:T(8,128)(2,1)} %reshape.175), calls=%async_computation.3 | async-start | bytes 4194304 | tf_op jit(solution)/shard_map/all_to_all | solution.py:31
  150.8 2.1 copy-start.2
  150.8 136.8 %reduce-scatter.8.cloned.1.call-start = ((), (), s32[]{:S(2)}) async-start(), calls=%async_computation.9 | async-start | bytes 2048000 | tf_op jit(solution)/shard_map/reduce_scatter | solution.py:61
  152.9 1.5 copy-start.1
  256.3 0.8 copy-start.3
  258.9 69.2 %reduce-scatter.10.cloned.1.call-start = ((), (), s32[]{:S(2)}) async-start(), calls=%async_computation.10 | async-start | bytes 2048000 | tf_op jit(solution)/shard_map/reduce_scatter | solution.py:64
  258.9 1.7 copy-start.5
  262.4 1.0 copy-start.4
  262.5 110.5 %reduce-scatter.16.cloned.1.call-start = ((), (), s32[]{:S(2)}) async-start(), calls=%async_computation.13 | async-start | bytes 589824
  293.8 43.3 %all-to-all-start.1 = ((bf16[32,2,3200]{2,1,0:T(2,128)(2,1)}), bf16[32,2,3200]{2,1,0:T(2,128)(2,1)S(1)}, u32[]{:S(2)}, u32[]{:S(2)}) async-start(bf16[32,2,3200]{2,1,0:T(2,128)(2,1)} %reshape.221), calls=%async_computation.2 | async-start | bytes 819200 | tf_op jit(solution)/shard_map/all_to_all | solution.py:69
  308.4 111.5 %reduce-scatter.12.cloned.1.call-start = ((), (), s32[]{:S(2)}) async-start(), calls=%async_computation.11 | async-start | bytes 589824 | tf_op jit(solution)/shard_map/reduce_scatter | solution.py:50
  337.1 135.5 %all-to-all-start.3 = ((bf16[32,2,3200]{2,1,0:T(2,128)(2,1)}), bf16[32,2,3200]{2,1,0:T(2,128)(2,1)}, u32[]{:S(2)}, u32[]{:S(2)}) async-start(bf16[32,2,3200]{2,1,0:T(2,128)(2,1)} %reshape.223), calls=%async_computation.5 | async-start | bytes 819200 | tf_op jit(solution)/shard_map/all_to_all | solution.py:72
  350.1 117.2 %reduce-scatter.14.cloned.1.call-start = ((), (), s32[]{:S(2)}) async-start(), calls=%async_computation.12 | async-start | bytes 589824 | tf_op jit(solution)/shard_map/reduce_scatter | solution.py:53
Sparse Core Ops, SparseCore 0:
  259.0 28.5 reduce-scatter.7
  291.4 36.5 reduce-scatter.9
  331.4 41.4 reduce-scatter.15
  376.5 43.2 reduce-scatter.11
  423.1 44.2 reduce-scatter.13
where the time goes:
time: 491 us; the launch traced here: 485 us
  waiting for transfers between devices  321 us (65%)
  starting transfers between devices  54.1 us (11%)
  local copies, waits for them, and re-layouts  50.1 us (10%)
  other arithmetic  25.6 us (5%)
  matrix products  20 us (4%)
  between operations  14.1 us (3%)
    all_to_all x1, waiting for transfers between devices, local(): lax.all_to_all(pack_slots(scaled), 'ep', split_axis=0, concat_axis=1, til...  94.1 us
    all_to_all x1, waiting for transfers between devices, local(): lax.all_to_all(pack_slots(route_rows), 'ep', split_axis=0, concat_axis=1,...  79.4 us
    reduce_scatter x1, waiting for transfers between devices, local(): lax.psum_scatter(up_terms.astype(jnp.bfloat16), 'dp', scatter_dimension=1...  46 us
    reduce_scatter x1, waiting for transfers between devices, local(): lax.psum_scatter(gate_terms.astype(jnp.bfloat16), 'dp', scatter_dimension...  45.2 us
    all_to_all x1, starting transfers between devices, local(): lax.all_to_all(pack_slots(route_rows), 'ep', split_axis=0, concat_axis=1,...  20.6 us
    unnamed x6, waiting for transfers between devices  20.2 us
    reduce_scatter x1, waiting for transfers between devices, local(): lax.psum_scatter(out_part.astype(jnp.bfloat16), 'tp', scatter_dimension=2...  17.9 us
    reduce_scatter x1, waiting for transfers between devices, local(): lax.psum_scatter(back_part.astype(jnp.bfloat16), 'tp', scatter_dimension=...  16.8 us
  transfers between devices with their start and end apart: 9, of which 8 were waited for; matrix products, arithmetic and copies ran while one was open for 13% of the time, Pallas kernels for 0%

commit v1 on v0

v1 whole, which is shorter than its diff:
```python
import jax
import jax.numpy as jnp
from jax import lax
from jax.experimental import pallas as pl
from jax.experimental.pallas import tpu as pltpu
from jax.sharding import PartitionSpec as P

MESH = pl.DeviceIdType.MESH
BF, F32 = jnp.bfloat16, jnp.float32

NZ, NX, NY = 16, 4, 8
TOK = 128
META = 16
CAP = 25
SLOT = 32
ROWS = 208
HALF = 112
Q = 256
GROUPS = ((2, -2, 3, -3), (4, -4, 5, -5), (6, -6, 7, -7), (1, -1, 8, 0))
INDEX = {(o, f): 8 * g + 2 * i + f for g, group in enumerate(GROUPS) for i, o in enumerate(group) for f in (0, 1)}


def dot(a, b):
    return jnp.dot(a, b, preferred_element_type=F32)


def dot_bt(a, b):
    return lax.dot_general(a, b, (((1,), (1,)), ((), ())), preferred_element_type=F32)


def dot_at(a, b):
    return lax.dot_general(a, b, (((0,), (0,)), ((), ())), preferred_element_type=F32)


def iota(shape, dim):
    return lax.broadcasted_iota(jnp.int32, shape, dim)


def one(condition):
    return jnp.where(condition, 1.0, 0.0)


def body(lat_ref, cot_ref, meta_ref, ids_ref, wg_ref, wu_ref, wd_ref,
         comb_ref, glat_ref, gg_ref, gu_ref, gd_ref,
         blocks, rows_in, parts, via, from_left, from_right, back_out, back_in, y_out, y_in,
         hid_s, dgu_s, prob_s, mask_s, pick_s, place_s, tokens_s, spread_s,
         ring_s, ring_r, gat_s, gat_r, sum_s, sum_r, ret_s, ret_r, y_s, y_r):
    ep, x, y = lax.axis_index("ep"), lax.axis_index("tp"), lax.axis_index("dp")
    z, core = ep // 2, lax.rem(ep, 2)

    def at_z(offset, flip):
        c = 1 - core if flip else core
        return (2 * lax.rem(z + offset + NZ, NZ) + c, x, y)

    def x_at(offset):
        return lax.rem(x + offset + NX, NX)

    def copy(src, dst, send, recv, device):
        return pltpu.make_async_remote_copy(
            src_ref=src, dst_ref=dst, send_sem=send, recv_sem=recv, device_id=device, device_id_type=MESH)

    right, left = (ep, x_at(1), y), (ep, x_at(-1), y)
    sent = []

    def go(c):
        c.start()
        sent.append(c)
        return c

    greeted = [at_z(1, 0), at_z(-1, 0), at_z(0, 1), right, left]
    greeted += [(ep, x, lax.rem(y + i, NY)) for i in range(1, NY)]
    barrier = pltpu.get_barrier_semaphore()
    for device in greeted:
        pl.semaphore_signal(barrier, inc=1, device_id=device, device_id_type=MESH)

    own = INDEX[0, 0]
    columns = pl.ds(pl.multiple_of(x * Q, Q), Q)
    blocks[own, 0:TOK, 0:Q] = lat_ref[:, columns]
    blocks[own, 0:TOK, Q:2 * Q] = cot_ref[:, columns]
    meta = meta_ref[...]
    hi = meta.astype(BF)
    rest = meta - hi.astype(F32)
    mid = rest.astype(BF)
    low = (rest - mid.astype(F32)).astype(BF)
    blocks[own, TOK:TOK + META, 0:128] = hi
    blocks[own, TOK:TOK + META, 128:256] = mid
    blocks[own, TOK:TOK + META, 256:384] = low
    blocks[own, TOK:TOK + META, 384:512] = jnp.zeros((META, 128), BF)
    pl.semaphore_wait(barrier, len(greeted))

    def ring_copy(offset, step):
        src, dst = INDEX[offset, 0], INDEX[offset + step, 0]
        return copy(blocks.at[src], blocks.at[dst], ring_s.at[dst], ring_r.at[dst], at_z(-step, 0))

    def twin_copy(offset):
        src, dst = INDEX[offset, 0], INDEX[offset, 1]
        return copy(blocks.at[src], blocks.at[dst], ring_s.at[dst], ring_r.at[dst], at_z(0, 1))

    arriving, twins = {}, {}
    arriving[1] = go(ring_copy(0, 1))
    arriving[-1] = go(ring_copy(0, -1))
    twins[0] = go(twin_copy(0))

    def ring(distance):
        for sign in (1, -1):
            offset = sign * distance
            if offset == -8:
                continue
            arriving[offset].wait_recv()
            if -7 < offset < 8:
                arriving[offset + sign] = go(ring_copy(offset, sign))
            twins[offset] = go(twin_copy(offset))

    ids = ids_ref[...]
    named = jnp.zeros((TOK, 32), F32)
    for k in range(6):
        named = named + one(ids[:, k:k + 1] == iota((TOK, 32), 1))
    below = one(iota((TOK, TOK), 0) > iota((TOK, TOK), 1)).astype(BF)
    rank = dot(below, named.astype(BF))
    rank = jnp.where(named > 0, rank, -1.0).astype(BF)
    first = 32 * iota((32, 32 * SLOT), 0)
    at = iota((32, 32 * SLOT), 1)
    wide = dot(rank, one((at >= first) & (at < first + SLOT)).astype(BF))
    tokens_s[...] = one(wide == (iota((TOK, 32 * SLOT), 1) & (SLOT - 1)).astype(F32)).astype(BF)
    for j in range(8):
        r, s = iota((SLOT, ROWS), 0), iota((SLOT, ROWS), 1)
        spread_s[j * SLOT:(j + 1) * SLOT, :] = one((s == r + CAP * j) & (r < CAP)).astype(BF)
    above = one(iota((TOK, TOK), 0) < iota((TOK, TOK), 1)).astype(BF)
    mine = ep.astype(F32)

    gathers, sums = {}, {}

    def span(g, part=None):
        if part is None:
            return pl.ds(g * ROWS, ROWS)
        return pl.ds(g * ROWS, HALF) if part == 0 else pl.ds(g * ROWS + HALF, ROWS - HALF)

    def gather_copy(g, i, q, part, device):
        ref = rows_in.at[q, span(g, part)]
        return copy(ref, ref, gat_s.at[6 * g + i], gat_r.at[6 * g + i], device)

    def select(g):
        for offset in GROUPS[g]:
            twins[offset].wait_recv()
        for j in range(8):
            held = blocks[8 * g + j, TOK:TOK + META, 0:384].astype(F32)
            held = held[:, 0:128] + held[:, 128:256] + held[:, 256:384]
            hit = held[0:8] == mine
            mask_s[j:j + 1, :] = jnp.sum(one(hit), axis=0, keepdims=True)
            pick_s[j:j + 1, :] = jnp.sum(jnp.where(hit, held[8:16], 0.0), axis=0, keepdims=True)
        mask = mask_s[...]
        place = dot(mask.astype(BF), above) + (CAP * iota((8, TOK), 0)).astype(F32)
        place_s[...] = jnp.where(mask > 0, place, -1.0)
        row = iota((ROWS, TOK), 0).astype(F32)
        prob = jnp.zeros((ROWS, TOK), F32)
        total = jnp.zeros((ROWS, 2 * Q), F32)
        for j in range(8):
            chosen = row == place_s[j:j + 1, :]
            prob = prob + jnp.where(chosen, pick_s[j:j + 1, :], 0.0)
            total = total + dot(one(chosen).astype(BF), blocks[8 * g + j, 0:TOK, :])
        prob = jnp.sum(prob, axis=1, keepdims=True)
        prob_s[span(g), :] = prob
        rows_in[x, span(g), 0:Q] = total[:, 0:Q].astype(BF)
        rows_in[x, span(g), Q:2 * Q] = (total[:, Q:2 * Q] * prob).astype(BF)
        gathers[g, 0] = go(gather_copy(g, 0, x, 0, right))
        gathers[g, 1] = go(gather_copy(g, 1, x, 1, left))
        gathers[g, 2] = go(gather_copy(g, 2, x, 1, right))
        gathers[g, 3] = go(gather_copy(g, 3, x, 0, left))

    def forward(g):
        gathers[g, 0].wait_recv()
        gathers[g, 4] = go(gather_copy(g, 4, x_at(-1), 0, right))
        gathers[g, 1].wait_recv()
        gathers[g, 5] = go(gather_copy(g, 5, x_at(1), 1, left))

    def sum_copy(g, i, src, dst, device):
        return copy(src, dst, sum_s.at[6 * g + i], sum_r.at[6 * g + i], device)

    def part_at(g, q, part):
        return parts.at[q, span(g, part)]

    def compute(g):
        for i in (2, 3, 4, 5):
            gathers[g, i].wait_recv()
        gate = jnp.zeros((ROWS, Q), F32)
        up = jnp.zeros((ROWS, Q), F32)
        d_hidden = jnp.zeros((ROWS, Q), F32)
        for q in range(NX):
            latent = rows_in[q, span(g), 0:Q]
            gate = gate + dot(latent, wg_ref[q * Q:(q + 1) * Q, :])
            up = up + dot(latent, wu_ref[q * Q:(q + 1) * Q, :])
            d_hidden = d_hidden + dot_bt(rows_in[q, span(g), Q:2 * Q], wd_ref[:, q * Q:(q + 1) * Q])
        sigmoid = jax.nn.sigmoid(gate)
        activated = gate * sigmoid
        hidden = (activated * up).astype(BF)
        slope = sigmoid * (1.0 + gate * (1.0 - sigmoid))
        d_gate = (d_hidden * up * slope).astype(BF)
        d_up = (d_hidden * activated).astype(BF)
        hid_s[span(g), :] = hidden
        dgu_s[span(g), 0:Q] = d_gate
        dgu_s[span(g), Q:2 * Q] = d_up
        for q in range(NX):
            parts[q, span(g), 0:Q] = dot(hidden, wd_ref[:, q * Q:(q + 1) * Q]).astype(BF)
            back = dot_bt(d_gate, wg_ref[q * Q:(q + 1) * Q, :]) + dot_bt(d_up, wu_ref[q * Q:(q + 1) * Q, :])
            parts[q, span(g), Q:2 * Q] = back.astype(BF)
        sums[g, 0] = go(sum_copy(g, 0, part_at(g, x_at(2), 0), via.at[span(g, 0)], right))
        sums[g, 1] = go(sum_copy(g, 1, part_at(g, x_at(2), 1), via.at[span(g, 1)], left))
        sums[g, 2] = go(sum_copy(g, 2, part_at(g, x_at(1), 1), from_left.at[span(g, 1)], right))
        sums[g, 3] = go(sum_copy(g, 3, part_at(g, x_at(-1), 0), from_right.at[span(g, 0)], left))

    def pass_on(g):
        for part, q, dst, device in ((0, x_at(1), from_left, right), (1, x_at(-1), from_right, left)):
            sums[g, part].wait_recv()
            here = span(g, part)
            parts[q, here, :] = (parts[q, here, :].astype(F32) + via[here, :].astype(F32)).astype(BF)
            sums[g, 4 + part] = go(sum_copy(g, 4 + part, part_at(g, q, part), dst.at[here], device))

    returns = []

    def give_back(g):
        for i in (2, 3, 4, 5):
            sums[g, i].wait_recv()
        here = span(g)
        total = parts[x, here, :].astype(F32) + from_left[here, :].astype(F32) + from_right[here, :].astype(F32)
        scaled = (total[:, 0:Q] * prob_s[here, :]).astype(BF)
        spread = spread_s[...]
        base = 8 * g * SLOT
        back_out[base:base + 8 * SLOT, 0:Q] = dot(spread, scaled).astype(BF)
        back_out[base:base + 8 * SLOT, Q:2 * Q] = dot(spread, total[:, Q:2 * Q].astype(BF)).astype(BF)
        target = pl.ds(pl.multiple_of(ep * SLOT, SLOT), SLOT)
        for offset in GROUPS[g]:
            for flip in (0, 1):
                i = INDEX[offset, flip]
                if i == own:
                    back_in[target, :] = back_out[i * SLOT:(i + 1) * SLOT, :]
                    continue
                returns.append(go(copy(back_out.at[pl.ds(i * SLOT, SLOT)], back_in.at[target],
                                       ret_s.at[i], ret_r.at[i], at_z(offset, flip))))

    trades = []

    def weight_gradients():
        for q in range(NX):
            both = dot_at(rows_in[q, :, 0:Q], dgu_s[...]).astype(BF)
            down = dot_at(hid_s[...], rows_in[q, :, Q:2 * Q]).astype(BF)
            for h in (0, 1):
                for c in range(4):
                    y_out[2 * q + h, c * 128:(c + 1) * 128, :] = both[h * 128:(h + 1) * 128, c * 128:(c + 1) * 128]
                y_out[2 * q + h, 512:768, :] = down[:, h * 128:(h + 1) * 128]
        for i in range(1, NY):
            to = lax.rem(y + i, NY)
            trades.append(go(copy(y_out.at[to], y_in.at[y], y_s.at[i], y_r.at[i], (ep, x, to))))

    ring(1)
    ring(2)
    ring(3)
    select(0)
    ring(4)
    forward(0)
    ring(5)
    select(1)
    ring(6)
    compute(0)
    forward(1)
    ring(7)
    ring(8)
    select(2)
    pass_on(0)
    compute(1)
    forward(2)
    select(3)
    give_back(0)
    pass_on(1)
    compute(2)
    forward(3)
    give_back(1)
    pass_on(2)
    compute(3)
    weight_gradients()
    give_back(2)
    pass_on(3)
    give_back(3)

    y_in[y] = y_out[y]
    for trade in trades:
        trade.wait_recv()
    sum_y = jnp.zeros((768, 128), F32)
    for i in range(NY):
        sum_y = sum_y + y_in[i].astype(F32)
    gg_ref[:, 0:128] = sum_y[0:128]
    gg_ref[:, 128:256] = sum_y[128:256]
    gu_ref[:, 0:128] = sum_y[256:384]
    gu_ref[:, 128:256] = sum_y[384:512]
    gd_ref[...] = sum_y[512:768]
    for c in returns:
        c.wait_recv()
    result = dot(tokens_s[...], back_in[...])
    comb_ref[...] = result[:, 0:Q].astype(BF)
    glat_ref[...] = result[:, Q:2 * Q].astype(BF)
    for c in sent:
        c.wait_send()


def local(latent, cotangent, expert_ids, route_probs, w_gate, w_up, w_down):
    meta = jnp.concatenate([
        expert_ids.T.astype(F32), jnp.full((2, TOK), -1.0, F32), route_probs.T, jnp.zeros((2, TOK), F32)], axis=0)
    vmem = pl.BlockSpec(memory_space=pltpu.VMEM)
    dma = pltpu.SemaphoreType.DMA
    comb, glat, gg, gu, gd = pl.pallas_call(
        body,
        out_shape=(
            jax.ShapeDtypeStruct((TOK, Q), BF), jax.ShapeDtypeStruct((TOK, Q), BF),
            jax.ShapeDtypeStruct((128, Q), F32), jax.ShapeDtypeStruct((128, Q), F32),
            jax.ShapeDtypeStruct((Q, 128), F32)),
        in_specs=[vmem] * 7,
        out_specs=(vmem,) * 5,
        scratch_shapes=[
            pltpu.VMEM((32, TOK + META, 2 * Q), BF),
            pltpu.VMEM((NX, 4 * ROWS, 2 * Q), BF),
            pltpu.VMEM((NX, 4 * ROWS, 2 * Q), BF),
            pltpu.VMEM((4 * ROWS, 2 * Q), BF),
            pltpu.VMEM((4 * ROWS, 2 * Q), BF),
            pltpu.VMEM((4 * ROWS, 2 * Q), BF),
            pltpu.VMEM((32 * SLOT, 2 * Q), BF),
            pltpu.VMEM((32 * SLOT, 2 * Q), BF),
            pltpu.VMEM((NY, 768, 128), BF),
            pltpu.VMEM((NY, 768, 128), BF),
            pltpu.VMEM((4 * ROWS, Q), BF),
            pltpu.VMEM((4 * ROWS, 2 * Q), BF),
            pltpu.VMEM((4 * ROWS, 1), F32),
            pltpu.VMEM((8, TOK), F32),
            pltpu.VMEM((8, TOK), F32),
            pltpu.VMEM((8, TOK), F32),
            pltpu.VMEM((TOK, 32 * SLOT), BF),
            pltpu.VMEM((8 * SLOT, ROWS), BF),
            dma((32,)), dma((32,)), dma((24,)), dma((24,)), dma((24,)), dma((24,)),
            dma((32,)), dma((32,)), dma((NY,)), dma((NY,)),
        ],
        compiler_params=pltpu.CompilerParams(collective_id=0, has_side_effects=True, vmem_limit_bytes=56 * 2**20),
        cost_estimate=pl.CostEstimate(flops=4 * 10**9, bytes_accessed=8 * 2**20, transcendentals=10**6),
        name="moe",
    )(latent, cotangent, meta, expert_ids, w_gate[0], w_up[0], w_down[0])
    return comb, glat, gg[None], gu[None], gd[None]


def solution(mesh):
    return jax.shard_map(
        local,
        mesh=mesh,
        in_specs=(
            P(("ep", "dp"), None), P(("ep", "dp"), None), P(("ep", "dp"), None), P(("ep", "dp"), None),
            P("ep", None, "tp"), P("ep", None, "tp"), P("ep", "tp", None),
        ),
        out_specs=(
            P(("ep", "dp"), "tp"), P(("ep", "dp"), "tp"), P("ep", "dp", "tp"), P("ep", "dp", "tp"), P("ep", "tp", "dp"),
        ),
        check_vma=False,
    )
```

time: 491 us -> 144 us (0.29); the launches traced: 485 us -> 143 us
  waiting for transfers between devices: 321 us -> 0 us
  Pallas kernels: 0 us -> 135 us
  starting transfers between devices: 54.1 us -> 0 us
  local copies, waits for them, and re-layouts: 50.1 us -> 6.8 us
  other arithmetic: 25.6 us -> 0.67 us
  matrix products: 20 us -> 0 us
  between operations: 14.1 us -> 0.68 us
    all_to_all x4 -> x0, waiting for transfers between devices: 175 us -> none  [the longest x1 94.1 us: local(): lax.all_to_all(pack_slots(scaled), 'ep', split_axis=0, concat_axis=1, til...]
    pallas_call x0 -> x1, Pallas kernels: none -> 135 us  [local(): pl.pallas_call(body, out_shape=(jax.ShapeDtypeStruct((TOK, Q), BF), jax.S...]
    reduce_scatter x4 -> x0, waiting for transfers between devices: 126 us -> none  [the longest x1 46 us: local(): lax.psum_scatter(up_terms.astype(jnp.bfloat16), 'dp', scatter_dimension=1...]
    all_to_all x4 -> x0, starting transfers between devices: 53.5 us -> none  [the longest x1 20.6 us: local(): lax.all_to_all(pack_slots(route_rows), 'ep', split_axis=0, concat_axis=1,...]
    unnamed x6 -> x0, waiting for transfers between devices: 20.2 us -> none
    dot_general x9 -> x0, matrix products: 20 us -> none  [the longest x1 3.62 us: local(): jnp.einsum('erl,efl->erf', grads_in, w_down, preferred_element_type=jnp.f...]
    scatter x1 -> x0, other arithmetic: 10.2 us -> none  [pack_slots(): empty.at[target].set(values).reshape(experts, capacity, values.shape[1])]
    reshape x5 -> x0, local copies, waits for them, and re-layouts: 7.1 us -> none  [the longest x1 3.7 us: local(): route_rows = jnp.repeat(latent, top_count, axis=0)]
  transfers between devices with their start and end apart: 9 -> 0, of which waited for: 8 -> 0; matrix products, arithmetic and copies ran while one was open for 13% -> 0% of each run, Pallas kernels for 0% -> 0%
where the time goes in v1:
time: 144 us; the launch traced here: 143 us
  Pallas kernels  135 us (94%)
  local copies, waits for them, and re-layouts  6.8 us (5%)
    pallas_call x1, Pallas kernels, local(): pl.pallas_call(body, out_shape=(jax.ShapeDtypeStruct((TOK, Q), BF), jax.S...  135 us
    unnamed x18, local copies, waits for them, and re-layouts  6.64 us

profile of v1, /device:TPU:1, one launch (start us, length us, event | category | flops | bytes accessed | tf_op | source)
XLA Modules:
  0.0 143.4 jit_solution(5861668822073290895)
XLA Ops:
  0.6 0.0 copy-start.4
  0.7 0.1 pad.1.clone
  0.7 0.1 pad.3.clone
  0.8 0.5 copy-done.4
  1.3 0.0 copy-start.5
  1.3 0.7 copy-done.5
  2.0 0.7 maximum_maximum_fusion.meta_ref
  2.7 0.7 copy.12.ids_ref
  3.4 135.3 %moe.1 = (bf16[128,256]{1,0:T(8,128)(2,1)}, bf16[128,256]{1,0:T(8,128)(2,1)}, f32[128,256]{1,0:T(8,128)}, f32[128,256]{1,0:T(8,128)}, f32[256,128]{1,0:T(8,128)}) custom-call(bf16[128,1024]{1,0:T(8,128)(2,1)} %lat_ref.1, bf16[128,1024]{1,0:T(8,128)(2,1)} %cot_ref.1, f32[16,128]{1,0:T(8,128)} %maximum_maximum_fusion.meta_ref, s32[128,6]{1,0:T(8,128)} %copy.12.ids_ref, ...), custom_call_target="tpu_custom_call" | custom-call | flops 4000000000 | bytes 8388608 | tf_op jit(solution)/shard_map/moe/pallas_call | solution.py:309
  138.7 0.0 copy-start.3
  138.7 0.0 copy-start.2
  138.7 1.5 %copy.18 = bf16[128,256]{1,0:T(8,128)(2,1)} copy(bf16[128,256]{1,0:T(8,128)(2,1)} %get-tuple-element.20) | data formatting | bytes 131072
  140.2 0.0 copy-done.3
  140.2 0.6 copy.19
  140.8 0.0 copy-done.2
  140.9 0.0 copy-start.1
  140.9 0.7 copy.20
  141.5 0.3 copy-done.1
  141.8 0.0 copy-start
  141.8 0.7 copy.21
  142.5 0.3 copy-done
  142.8 0.7 copy.22
  (3 shorter events, 0.0 us)
Async XLA Ops:
  0.6 0.7 copy-start.4
  1.3 0.7 copy-start.5
  138.7 1.5 %copy-start.3 = (bf16[128,256]{1,0:T(8,128)(2,1)S(1)}, bf16[128,256]{1,0:T(8,128)(2,1)}, u32[]{:S(2)}) copy-start(bf16[128,256]{1,0:T(8,128)(2,1)} %get-tuple-element.21) | copy-start | bytes 196612
  138.7 2.2 %copy-start.2 = (f32[128,256]{1,0:T(8,128)S(1)}, f32[128,256]{1,0:T(8,128)}, u32[]{:S(2)}) copy-start(f32[128,256]{1,0:T(8,128)} %get-tuple-element.12) | copy-start | bytes 393220
  140.9 1.0 copy-start.1
  141.8 1.0 copy-start

commit v2 on v1

v2 whole, which is shorter than its diff:
```python
import jax
import jax.numpy as jnp
from jax import lax
from jax.experimental import pallas as pl
from jax.experimental.pallas import tpu as pltpu
from jax.sharding import PartitionSpec as P

MESH = pl.DeviceIdType.MESH
BF, F32 = jnp.bfloat16, jnp.float32

NZ, NX, NY = 16, 4, 8
TOK = 128
META = 16
CAP = 25
SLOT = 112
Q = 256
CHUNKS = (0, 64, TOK + META)
GROUPS = ((2, -2), (3, -3, 4, -4), (5, -5, 6, -6), (7, -7, 8), (1, -1, 0))
FIRST = [2 * sum(len(group) for group in GROUPS[:g]) for g in range(len(GROUPS) + 1)]
INDEX = {(o, f): FIRST[g] + 2 * i + f for g, group in enumerate(GROUPS) for i, o in enumerate(group) for f in (0, 1)}
BLOCKS = [2 * len(group) for group in GROUPS]
MOST = max(BLOCKS)
ROWS = [-(-CAP * n // 16) * 16 for n in BLOCKS]
HALF = [-(-rows // 32) * 16 for rows in ROWS]
START = [sum(ROWS[:g]) for g in range(len(GROUPS) + 1)]
ALL = START[-1]
ORDER = "r1.0 r1.1 r2.0 s4 r2.1 r3.0 s0 r3.1 r4.0 f4 f0 r4.1 r5.0 s1 r5.1 c0 r6.0 f1 r6.1 r7.0 p0 s2 g0 f2 c1 r7.1 p1 c2 r8.0 r8.1 g1 p2 s3 g2 f3 c4 c3 w0 p4 p3 g4 g3"
FIRST_COMPUTED = int(ORDER[ORDER.index("c") + 1])


def dot(a, b):
    return jnp.dot(a, b, preferred_element_type=F32)


def dot_bt(a, b):
    return lax.dot_general(a, b, (((1,), (1,)), ((), ())), preferred_element_type=F32)


def dot_at(a, b):
    return lax.dot_general(a, b, (((0,), (0,)), ((), ())), preferred_element_type=F32)


def iota(shape, dim):
    return lax.broadcasted_iota(jnp.int32, shape, dim)


def one(condition):
    return jnp.where(condition, 1.0, 0.0)


def body(lat_ref, cot_ref, ids_ref, probs_ref, wg_hbm, wu_hbm, wd_hbm,
         comb_ref, glat_ref, gg_ref, gu_ref, gd_ref,
         blocks, rows_in, parts, via, from_left, from_right, back_out, back_in, y_out, y_in,
         hid_s, dgu_s, prob_s, mask_s, pick_s, place_s, tokens_s, spread_s,
         wg_ref, wu_ref, wd_ref, load_s, ring_s, ring_r, gat_s, gat_r, sum_s, sum_r, ret_s, ret_r, y_s, y_r):
    ep, x, y = lax.axis_index("ep"), lax.axis_index("tp"), lax.axis_index("dp")
    z, core = ep // 2, lax.rem(ep, 2)

    def at_z(offset, flip):
        c = 1 - core if flip else core
        return (2 * lax.rem(z + offset + NZ, NZ) + c, x, y)

    def x_at(offset):
        return lax.rem(x + offset + NX, NX)

    def copy(src, dst, send, recv, device):
        return pltpu.make_async_remote_copy(
            src_ref=src, dst_ref=dst, send_sem=send, recv_sem=recv, device_id=device, device_id_type=MESH)

    right, left = (ep, x_at(1), y), (ep, x_at(-1), y)
    sent = []

    def go(c):
        c.start()
        sent.append(c)
        return c

    own = INDEX[0, 0]
    columns = pl.ds(pl.multiple_of(x * Q, Q), Q)
    loads = [
        pltpu.make_async_copy(lat_ref.at[:, columns], blocks.at[own, pl.ds(0, TOK), pl.ds(0, Q)], load_s.at[0]),
        pltpu.make_async_copy(cot_ref.at[:, columns], blocks.at[own, pl.ds(0, TOK), pl.ds(Q, Q)], load_s.at[1]),
        pltpu.make_async_copy(wg_hbm, wg_ref, load_s.at[2]),
        pltpu.make_async_copy(wu_hbm, wu_ref, load_s.at[3]),
        pltpu.make_async_copy(wd_hbm, wd_ref, load_s.at[4]),
    ]
    for c in loads:
        c.start()

    greeted = [at_z(1, 0), at_z(-1, 0), at_z(0, 1), right, left]
    greeted += [(ep, x, lax.rem(y + i, NY)) for i in range(1, NY)]
    barrier = pltpu.get_barrier_semaphore()
    for device in greeted:
        pl.semaphore_signal(barrier, inc=1, device_id=device, device_id_type=MESH)

    meta = jnp.concatenate([
        ids_ref[...].astype(F32), jnp.full((2, TOK), -1.0, F32), probs_ref[...], jnp.zeros((2, TOK), F32)], axis=0)
    hi = meta.astype(BF)
    rest = meta - hi.astype(F32)
    mid = rest.astype(BF)
    low = (rest - mid.astype(F32)).astype(BF)
    blocks[own, TOK:TOK + META, 0:128] = hi
    blocks[own, TOK:TOK + META, 128:256] = mid
    blocks[own, TOK:TOK + META, 256:384] = low
    blocks[own, TOK:TOK + META, 384:512] = jnp.zeros((META, 128), BF)
    for c in loads[:2]:
        c.wait()
    pl.semaphore_wait(barrier, len(greeted))

    def ring_copy(offset, step, c):
        src, dst, part = INDEX[offset, 0], INDEX[offset + step, 0], pl.ds(CHUNKS[c], CHUNKS[c + 1] - CHUNKS[c])
        return copy(blocks.at[src, part], blocks.at[dst, part], ring_s.at[dst, c], ring_r.at[dst, c], at_z(-step, 0))

    def twin_copy(offset, c):
        src, dst, part = INDEX[offset, 0], INDEX[offset, 1], pl.ds(CHUNKS[c], CHUNKS[c + 1] - CHUNKS[c])
        return copy(blocks.at[src, part], blocks.at[dst, part], ring_s.at[dst, c], ring_r.at[dst, c], at_z(0, 1))

    arriving, twins = {}, {}
    pieces = range(len(CHUNKS) - 1)
    for c in pieces:
        arriving[1, c] = go(ring_copy(0, 1, c))
        arriving[-1, c] = go(ring_copy(0, -1, c))
    for c in pieces:
        twins[0, c] = go(twin_copy(0, c))

    def ring(distance, only=None):
        for c in pieces if only is None else (only,):
            for sign in (1, -1):
                offset = sign * distance
                if offset == -8:
                    continue
                arriving[offset, c].wait_recv()
                if -7 < offset < 8:
                    arriving[offset + sign, c] = go(ring_copy(offset, sign, c))
                twins[offset, c] = go(twin_copy(offset, c))

    ids = ids_ref[...]
    named = jnp.zeros((32, TOK), F32)
    for k in range(6):
        named = named + one(ids[k:k + 1, :] == iota((32, TOK), 0))
    above = one(iota((TOK, TOK), 0) < iota((TOK, TOK), 1)).astype(BF)
    rank = dot(named.astype(BF), above)
    rank = jnp.where(named > 0, rank, -1024.0).astype(BF)
    first = SLOT * iota((32, 32 * SLOT), 0)
    at = iota((32, 32 * SLOT), 1)
    inside = (at >= first) & (at < first + SLOT)
    wide = dot_at(rank, one(inside).astype(BF))
    within = jnp.sum(jnp.where(inside, at - first, 0), axis=0, keepdims=True).astype(F32)
    for c in range(4):
        tokens_s[c] = one(wide + float(CAP * c) == within).astype(BF)
        for j in range(MOST):
            r, s = iota((SLOT, max(ROWS)), 0) - CAP * c, iota((SLOT, max(ROWS)), 1)
            spread_s[c, j * SLOT:(j + 1) * SLOT, :] = one((s == r + CAP * j) & (r >= 0) & (r < CAP)).astype(BF)
    mine = ep.astype(F32)

    gathers, sums = {}, {}

    def span(g, part=None):
        if part is None:
            return pl.ds(START[g], ROWS[g])
        return pl.ds(START[g], HALF[g]) if part == 0 else pl.ds(START[g] + HALF[g], ROWS[g] - HALF[g])

    def gather_copy(g, i, q, part, device):
        ref = rows_in.at[q, span(g, part)]
        return copy(ref, ref, gat_s.at[6 * g + i], gat_r.at[6 * g + i], device)

    def select(g):
        count, rows = BLOCKS[g], ROWS[g]
        for offset in GROUPS[g]:
            for c in pieces:
                twins[offset, c].wait_recv()
        for j in range(count):
            held = blocks[FIRST[g] + j, TOK:TOK + META, 0:384].astype(F32)
            held = held[:, 0:128] + held[:, 128:256] + held[:, 256:384]
            hit = held[0:8] == mine
            mask_s[j:j + 1, :] = jnp.sum(one(hit), axis=0, keepdims=True)
            pick_s[j:j + 1, :] = jnp.sum(jnp.where(hit, held[8:16], 0.0), axis=0, keepdims=True)
        mask = mask_s[0:count, :]
        place = dot(mask.astype(BF), above) + (CAP * iota((count, TOK), 0)).astype(F32)
        place_s[0:count, :] = jnp.where(mask > 0, place, -1.0)
        row = iota((rows, TOK), 0).astype(F32)
        prob = jnp.zeros((rows, TOK), F32)
        total = jnp.zeros((rows, 2 * Q), F32)
        for j in range(count):
            chosen = row == place_s[j:j + 1, :]
            prob = prob + jnp.where(chosen, pick_s[j:j + 1, :], 0.0)
            total = total + dot(one(chosen).astype(BF), blocks[FIRST[g] + j, 0:TOK, :])
        prob = jnp.sum(prob, axis=1, keepdims=True)
        prob_s[span(g), :] = prob
        rows_in[x, span(g), 0:Q] = total[:, 0:Q].astype(BF)
        rows_in[x, span(g), Q:2 * Q] = (total[:, Q:2 * Q] * prob).astype(BF)
        gathers[g, 0] = go(gather_copy(g, 0, x, 0, right))
        gathers[g, 1] = go(gather_copy(g, 1, x, 1, left))
        gathers[g, 2] = go(gather_copy(g, 2, x, 1, right))
        gathers[g, 3] = go(gather_copy(g, 3, x, 0, left))

    def forward(g):
        gathers[g, 0].wait_recv()
        gathers[g, 4] = go(gather_copy(g, 4, x_at(-1), 0, right))
        gathers[g, 1].wait_recv()
        gathers[g, 5] = go(gather_copy(g, 5, x_at(1), 1, left))

    def sum_copy(g, i, src, dst, device):
        return copy(src, dst, sum_s.at[6 * g + i], sum_r.at[6 * g + i], device)

    def part_at(g, q, part):
        return parts.at[q, span(g, part)]

    def compute(g):
        for i in (2, 3, 4, 5):
            gathers[g, i].wait_recv()
        if g == FIRST_COMPUTED:
            for c in loads[2:]:
                c.wait()
        gate = jnp.zeros((ROWS[g], Q), F32)
        up = jnp.zeros((ROWS[g], Q), F32)
        d_hidden = jnp.zeros((ROWS[g], Q), F32)
        for q in range(NX):
            latent = rows_in[q, span(g), 0:Q]
            gate = gate + dot(latent, wg_ref[q * Q:(q + 1) * Q, :])
            up = up + dot(latent, wu_ref[q * Q:(q + 1) * Q, :])
            d_hidden = d_hidden + dot_bt(rows_in[q, span(g), Q:2 * Q], wd_ref[:, q * Q:(q + 1) * Q])
        sigmoid = jax.nn.sigmoid(gate)
        activated = gate * sigmoid
        hidden = (activated * up).astype(BF)
        slope = sigmoid * (1.0 + gate * (1.0 - sigmoid))
        d_gate = (d_hidden * up * slope).astype(BF)
        d_up = (d_hidden * activated).astype(BF)
        hid_s[span(g), :] = hidden
        dgu_s[span(g), 0:Q] = d_gate
        dgu_s[span(g), Q:2 * Q] = d_up
        for q in range(NX):
            parts[q, span(g), 0:Q] = dot(hidden, wd_ref[:, q * Q:(q + 1) * Q]).astype(BF)
            back = dot_bt(d_gate, wg_ref[q * Q:(q + 1) * Q, :]) + dot_bt(d_up, wu_ref[q * Q:(q + 1) * Q, :])
            parts[q, span(g), Q:2 * Q] = back.astype(BF)
        sums[g, 0] = go(sum_copy(g, 0, part_at(g, x_at(2), 0), via.at[span(g, 0)], right))
        sums[g, 1] = go(sum_copy(g, 1, part_at(g, x_at(2), 1), via.at[span(g, 1)], left))
        sums[g, 2] = go(sum_copy(g, 2, part_at(g, x_at(1), 1), from_left.at[span(g, 1)], right))
        sums[g, 3] = go(sum_copy(g, 3, part_at(g, x_at(-1), 0), from_right.at[span(g, 0)], left))

    def pass_on(g):
        for part, q, dst, device in ((0, x_at(1), from_left, right), (1, x_at(-1), from_right, left)):
            sums[g, part].wait_recv()
            here = span(g, part)
            parts[q, here, :] = (parts[q, here, :].astype(F32) + via[here, :].astype(F32)).astype(BF)
            sums[g, 4 + part] = go(sum_copy(g, 4 + part, part_at(g, q, part), dst.at[here], device))

    returns = []

    def give_back(g):
        for i in (2, 3, 4, 5):
            sums[g, i].wait_recv()
        here = span(g)
        total = parts[x, here, :].astype(F32) + from_left[here, :].astype(F32) + from_right[here, :].astype(F32)
        scaled = (total[:, 0:Q] * prob_s[here, :]).astype(BF)
        plain = total[:, Q:2 * Q].astype(BF)
        size = BLOCKS[g] * SLOT
        packed = jnp.zeros((size, 128), F32)
        for c, values in enumerate((scaled[:, 0:128], scaled[:, 128:256], plain[:, 0:128], plain[:, 128:256])):
            packed = packed + dot(spread_s[c, 0:size, 0:ROWS[g]], values)
        back_out[FIRST[g] * SLOT:FIRST[g] * SLOT + size, :] = packed.astype(BF)
        target = pl.ds(pl.multiple_of(ep * SLOT, SLOT), SLOT)
        for offset in GROUPS[g]:
            for flip in (0, 1):
                i = INDEX[offset, flip]
                if i == own:
                    back_in[target, :] = back_out[i * SLOT:(i + 1) * SLOT, :]
                    continue
                returns.append(go(copy(back_out.at[pl.ds(i * SLOT, SLOT)], back_in.at[target],
                                       ret_s.at[i], ret_r.at[i], at_z(offset, flip))))

    trades = []

    def weight_gradients(_):
        for q in range(NX):
            both = dot_at(rows_in[q, :, 0:Q], dgu_s[...]).astype(BF)
            down = dot_at(hid_s[...], rows_in[q, :, Q:2 * Q]).astype(BF)
            for h in (0, 1):
                for c in range(4):
                    y_out[2 * q + h, c * 128:(c + 1) * 128, :] = both[h * 128:(h + 1) * 128, c * 128:(c + 1) * 128]
                y_out[2 * q + h, 512:768, :] = down[:, h * 128:(h + 1) * 128]
        for i in range(1, NY):
            to = lax.rem(y + i, NY)
            trades.append(go(copy(y_out.at[to], y_in.at[y], y_s.at[i], y_r.at[i], (ep, x, to))))

    steps = dict(r=ring, s=select, f=forward, c=compute, p=pass_on, g=give_back, w=weight_gradients)
    for word in ORDER.split():
        steps[word[0]](*[int(n) for n in word[1:].split(".")])

    y_in[y] = y_out[y]
    for trade in trades:
        trade.wait_recv()
    sum_y = jnp.zeros((768, 128), F32)
    for i in range(NY):
        sum_y = sum_y + y_in[i].astype(F32)
    gg_ref[0, :, 0:128] = sum_y[0:128]
    gg_ref[0, :, 128:256] = sum_y[128:256]
    gu_ref[0, :, 0:128] = sum_y[256:384]
    gu_ref[0, :, 128:256] = sum_y[384:512]
    gd_ref[0] = sum_y[512:768]
    for c in returns:
        c.wait_recv()
    for c, (ref, half) in enumerate(((comb_ref, 0), (comb_ref, 1), (glat_ref, 0), (glat_ref, 1))):
        ref[:, half * 128:(half + 1) * 128] = dot(tokens_s[c], back_in[...]).astype(BF)
    for c in sent:
        c.wait_send()


def local(latent, cotangent, expert_ids, route_probs, w_gate, w_up, w_down):
    vmem, anywhere = pl.BlockSpec(memory_space=pltpu.VMEM), pl.BlockSpec(memory_space=pl.ANY)
    dma = pltpu.SemaphoreType.DMA
    groups = len(GROUPS)
    shapes = (
        jax.ShapeDtypeStruct((TOK, Q), BF), jax.ShapeDtypeStruct((TOK, Q), BF),
        jax.ShapeDtypeStruct((1, 128, Q), F32), jax.ShapeDtypeStruct((1, 128, Q), F32),
        jax.ShapeDtypeStruct((1, Q, 128), F32))
    results = pl.pallas_call(
        body,
        out_shape=shapes,
        in_specs=[anywhere, anywhere, vmem, vmem, anywhere, anywhere, anywhere],
        out_specs=(vmem,) * 5,
        scratch_shapes=[
            pltpu.VMEM((32, TOK + META, 2 * Q), BF),
            pltpu.VMEM((NX, ALL, 2 * Q), BF),
            pltpu.VMEM((NX, ALL, 2 * Q), BF),
            pltpu.VMEM((ALL, 2 * Q), BF),
            pltpu.VMEM((ALL, 2 * Q), BF),
            pltpu.VMEM((ALL, 2 * Q), BF),
            pltpu.VMEM((32 * SLOT, 128), BF),
            pltpu.VMEM((32 * SLOT, 128), BF),
            pltpu.VMEM((NY, 768, 128), BF),
            pltpu.VMEM((NY, 768, 128), BF),
            pltpu.VMEM((ALL, Q), BF),
            pltpu.VMEM((ALL, 2 * Q), BF),
            pltpu.VMEM((ALL, 1), F32),
            pltpu.VMEM((16, TOK), F32),
            pltpu.VMEM((16, TOK), F32),
            pltpu.VMEM((16, TOK), F32),
            pltpu.VMEM((4, TOK, 32 * SLOT), BF),
            pltpu.VMEM((4, MOST * SLOT, max(ROWS)), BF),
            pltpu.VMEM((4 * Q, Q), BF), pltpu.VMEM((4 * Q, Q), BF), pltpu.VMEM((Q, 4 * Q), BF),
            dma((5,)), dma((32, len(CHUNKS) - 1)), dma((32, len(CHUNKS) - 1)),
            dma((6 * groups,)), dma((6 * groups,)), dma((6 * groups,)), dma((6 * groups,)),
            dma((32,)), dma((32,)), dma((NY,)), dma((NY,)),
        ],
        compiler_params=pltpu.CompilerParams(collective_id=0, has_side_effects=True, vmem_limit_bytes=56 * 2**20),
        cost_estimate=pl.CostEstimate(flops=4 * 10**9, bytes_accessed=8 * 2**20, transcendentals=10**6),
        name="moe",
    )(latent, cotangent, expert_ids.T, route_probs.T, w_gate[0], w_up[0], w_down[0])
    return pl.pallas_call(
        hand_over,
        out_shape=shapes,
        in_specs=[vmem] * 5,
        out_specs=(vmem,) * 5,
        name="results",
    )(*results)


def hand_over(*refs):
    for i in range(5):
        refs[5 + i][...] = refs[i][...]


def solution(mesh):
    return jax.shard_map(
        local,
        mesh=mesh,
        in_specs=(
            P(("ep", "dp"), None), P(("ep", "dp"), None), P(("ep", "dp"), None), P(("ep", "dp"), None),
            P("ep", None, "tp"), P("ep", None, "tp"), P("ep", "tp", None),
        ),
        out_specs=(
            P(("ep", "dp"), "tp"), P(("ep", "dp"), "tp"), P("ep", "dp", "tp"), P("ep", "dp", "tp"), P("ep", "tp", "dp"),
        ),
        check_vma=False,
    )
```

time: 144 us -> 128 us (0.89)
  Pallas kernels: 135 us -> 126 us
  local copies, waits for them, and re-layouts: 6.8 us -> 0 us
    pallas_call x1 -> x2, Pallas kernels: 135 us -> 126 us  [the longest x1 124 us: local(): pl.pallas_call(body, out_shape=shapes, in_specs=[anywhere, anywhere, vmem...]
    unnamed x18 -> x0, local copies, waits for them, and re-layouts: 6.64 us -> none
where the time goes in v2:
time: 128 us; the launch traced here: 127 us
  Pallas kernels  126 us (98%)
    pallas_call x1, Pallas kernels, local(): pl.pallas_call(body, out_shape=shapes, in_specs=[anywhere, anywhere, vmem...  124 us

profile of v2, /device:TPU:1, one launch (start us, length us, event | category | flops | bytes accessed | tf_op | source)
XLA Modules:
  0.0 126.6 jit_solution(4149484704162399888)
XLA Ops:
  0.6 124.1 %moe.1 = (bf16[128,256]{1,0:T(8,128)(2,1)}, bf16[128,256]{1,0:T(8,128)(2,1)}, f32[1,128,256]{2,1,0:T(8,128)}, f32[1,128,256]{2,1,0:T(8,128)}, f32[1,256,128]{2,1,0:T(8,128)}) custom-call(bf16[128,1024]{1,0:T(8,128)(2,1)} %lat_ref.1, bf16[128,1024]{1,0:T(8,128)(2,1)} %cot_ref.1, s32[6,128]{1,0:T(8,128)} %bitcast.8, f32[6,128]{1,0:T(8,128)} %bitcast.9, ...), custom_call_target="tpu_custom_call" | custom-call | flops 4000000000 | bytes 8388608 | tf_op jit(solution)/shard_map/moe/pallas_call | solution.py:317
  124.7 1.9 %results.1 = (bf16[128,256]{1,0:T(8,128)(2,1)}, bf16[128,256]{1,0:T(8,128)(2,1)}, f32[1,128,256]{2,1,0:T(8,128)}, f32[1,128,256]{2,1,0:T(8,128)}, f32[1,256,128]{2,1,0:T(8,128)}) custom-call(bf16[128,256]{1,0:T(8,128)(2,1)} %get-tuple-element.10.refs_0_, bf16[128,256]{1,0:T(8,128)(2,1)} %get-tuple-element.11.refs_1_, ...), custom_call_target="tpu_custom_call" | custom-call | tf_op jit(solution)/shard_map/results/pallas_call | solution.py:350

commit v3 on v2

--- a/solution.py
+++ b/solution.py
@@ -15,7 +15,7 @@
 SLOT = 112
 Q = 256
 CHUNKS = (0, 64, TOK + META)
-GROUPS = ((2, -2), (3, -3, 4, -4), (5, -5, 6, -6), (7, -7, 8), (1, -1, 0))
+GROUPS = ((2, -2, 3, -3), (8, 7, -7), (5, -5, 6, -6), (4, -4), (1, -1, 0))
 FIRST = [2 * sum(len(group) for group in GROUPS[:g]) for g in range(len(GROUPS) + 1)]
 INDEX = {(o, f): FIRST[g] + 2 * i + f for g, group in enumerate(GROUPS) for i, o in enumerate(group) for f in (0, 1)}
 BLOCKS = [2 * len(group) for group in GROUPS]
@@ -24,7 +24,7 @@
 HALF = [-(-rows // 32) * 16 for rows in ROWS]
 START = [sum(ROWS[:g]) for g in range(len(GROUPS) + 1)]
 ALL = START[-1]
-ORDER = "r1.0 r1.1 r2.0 s4 r2.1 r3.0 s0 r3.1 r4.0 f4 f0 r4.1 r5.0 s1 r5.1 c0 r6.0 f1 r6.1 r7.0 p0 s2 g0 f2 c1 r7.1 p1 c2 r8.0 r8.1 g1 p2 s3 g2 f3 c4 c3 w0 p4 p3 g4 g3"
+ORDER = "r1.0 r1.1 r2.0 r2.1 s4 r3.0 r3.1 f4 r4.0 s0 r4.1 r5.0 s3 r5.1 r6.0 f0 r6.1 r7.0 f3 s2 r7.1 r8.0 r8.1 f2 s1 c2 p2 f1 c3 c4 g2 c1 p3 c0 w0 g3 p0 p1 g0 p4 g1 g4"
 FIRST_COMPUTED = int(ORDER[ORDER.index("c") + 1])
 
 
@@ -108,7 +108,8 @@
     pl.semaphore_wait(barrier, len(greeted))
 
     def ring_copy(offset, step, c):
-        src, dst, part = INDEX[offset, 0], INDEX[offset + step, 0], pl.ds(CHUNKS[c], CHUNKS[c + 1] - CHUNKS[c])
+        src, dst = INDEX[offset, 0], INDEX[8 if offset + step == -8 else offset + step, 0]
+        part = pl.ds(CHUNKS[c], CHUNKS[c + 1] - CHUNKS[c])
         return copy(blocks.at[src, part], blocks.at[dst, part], ring_s.at[dst, c], ring_r.at[dst, c], at_z(-step, 0))
 
     def twin_copy(offset, c):
@@ -125,13 +126,13 @@
 
     def ring(distance, only=None):
         for c in pieces if only is None else (only,):
-            for sign in (1, -1):
-                offset = sign * distance
-                if offset == -8:
-                    continue
+            for offset in (distance, -distance) if distance < 8 else (8,):
                 arriving[offset, c].wait_recv()
-                if -7 < offset < 8:
-                    arriving[offset + sign, c] = go(ring_copy(offset, sign, c))
+                step = 1 if offset > 0 else -1
+                if distance < 7:
+                    arriving[offset + step, c] = go(ring_copy(offset, step, c))
+                elif distance == 7 and step == 1 - 2 * (c % 2):
+                    arriving[8, c] = go(ring_copy(offset, step, c))
                 twins[offset, c] = go(twin_copy(offset, c))
 
     ids = ids_ref[...]

time: 128 us -> 123 us (0.961)
  Pallas kernels: 126 us -> 121 us
    pallas_call x1, Pallas kernels: 124 us -> 119 us  [local(): pl.pallas_call(body, out_shape=shapes, in_specs=[anywhere, anywhere, vmem...]
where the time goes in v3:
time: 123 us; the launch traced here: 122 us
  Pallas kernels  121 us (98%)
    pallas_call x1, Pallas kernels, local(): pl.pallas_call(body, out_shape=shapes, in_specs=[anywhere, anywhere, vmem...  119 us

profile of v3, /device:TPU:1, one launch (start us, length us, event | category | flops | bytes accessed | tf_op | source)
XLA Modules:
  0.0 121.5 jit_solution(3697190988834218637)
XLA Ops:
  0.6 119.0 %moe.1 = (bf16[128,256]{1,0:T(8,128)(2,1)}, bf16[128,256]{1,0:T(8,128)(2,1)}, f32[1,128,256]{2,1,0:T(8,128)}, f32[1,128,256]{2,1,0:T(8,128)}, f32[1,256,128]{2,1,0:T(8,128)}) custom-call(bf16[128,1024]{1,0:T(8,128)(2,1)} %lat_ref.1, bf16[128,1024]{1,0:T(8,128)(2,1)} %cot_ref.1, s32[6,128]{1,0:T(8,128)} %bitcast.8, f32[6,128]{1,0:T(8,128)} %bitcast.9, ...), custom_call_target="tpu_custom_call" | custom-call | flops 4000000000 | bytes 8388608 | tf_op jit(solution)/shard_map/moe/pallas_call | solution.py:318
  119.6 1.9 %results.1 = (bf16[128,256]{1,0:T(8,128)(2,1)}, bf16[128,256]{1,0:T(8,128)(2,1)}, f32[1,128,256]{2,1,0:T(8,128)}, f32[1,128,256]{2,1,0:T(8,128)}, f32[1,256,128]{2,1,0:T(8,128)}) custom-call(bf16[128,256]{1,0:T(8,128)(2,1)} %get-tuple-element.10.refs_0_, bf16[128,256]{1,0:T(8,128)(2,1)} %get-tuple-element.11.refs_1_, ...), custom_call_target="tpu_custom_call" | custom-call | tf_op jit(solution)/shard_map/results/pallas_call | solution.py:351

commit v4 on v3

--- a/solution.py
+++ b/solution.py
@@ -15,7 +15,7 @@
 SLOT = 112
 Q = 256
 CHUNKS = (0, 64, TOK + META)
-GROUPS = ((2, -2, 3, -3), (8, 7, -7), (5, -5, 6, -6), (4, -4), (1, -1, 0))
+GROUPS = ((1, -1, 0), (2, -2, 3, -3), (4, -4, 5, -5), (6, -6), (7, -7, 8))
 FIRST = [2 * sum(len(group) for group in GROUPS[:g]) for g in range(len(GROUPS) + 1)]
 INDEX = {(o, f): FIRST[g] + 2 * i + f for g, group in enumerate(GROUPS) for i, o in enumerate(group) for f in (0, 1)}
 BLOCKS = [2 * len(group) for group in GROUPS]
@@ -24,7 +24,7 @@
 HALF = [-(-rows // 32) * 16 for rows in ROWS]
 START = [sum(ROWS[:g]) for g in range(len(GROUPS) + 1)]
 ALL = START[-1]
-ORDER = "r1.0 r1.1 r2.0 r2.1 s4 r3.0 r3.1 f4 r4.0 s0 r4.1 r5.0 s3 r5.1 r6.0 f0 r6.1 r7.0 f3 s2 r7.1 r8.0 r8.1 f2 s1 c2 p2 f1 c3 c4 g2 c1 p3 c0 w0 g3 p0 p1 g0 p4 g1 g4"
+ORDER = "r1.0 r1.1 r2.0 r2.1 s0 r3.0 r3.1 f0 r4.0 s1 r4.1 r5.0 r5.1 f1 s2 r6.0 c1 r6.1 s3 r7.0 r7.1 r8.0 p1 r8.1 f3 s4 c3 f4 g1 f2 p3 c4 c0 g3 p4 c2 w0 p0 g4 g0 p2 g2"
 FIRST_COMPUTED = int(ORDER[ORDER.index("c") + 1])
 
 

time: 123 us -> 125 us (1.016)
  Pallas kernels: 121 us -> 124 us
    pallas_call x1, Pallas kernels: 119 us -> 122 us  [local(): pl.pallas_call(body, out_shape=shapes, in_specs=[anywhere, anywhere, vmem...]
where the time goes in v4:
time: 125 us; the launch traced here: 124 us
  Pallas kernels  124 us (99%)
    pallas_call x1, Pallas kernels, local(): pl.pallas_call(body, out_shape=shapes, in_specs=[anywhere, anywhere, vmem...  122 us

profile of v4, /device:TPU:1, one launch (start us, length us, event | category | flops | bytes accessed | tf_op | source)
XLA Modules:
  0.0 124.3 jit_solution(16639204738426707606)
XLA Ops:
  0.6 121.8 %moe.1 = (bf16[128,256]{1,0:T(8,128)(2,1)}, bf16[128,256]{1,0:T(8,128)(2,1)}, f32[1,128,256]{2,1,0:T(8,128)}, f32[1,128,256]{2,1,0:T(8,128)}, f32[1,256,128]{2,1,0:T(8,128)}) custom-call(bf16[128,1024]{1,0:T(8,128)(2,1)} %lat_ref.1, bf16[128,1024]{1,0:T(8,128)(2,1)} %cot_ref.1, s32[6,128]{1,0:T(8,128)} %bitcast.8, f32[6,128]{1,0:T(8,128)} %bitcast.9, ...), custom_call_target="tpu_custom_call" | custom-call | flops 4000000000 | bytes 8388608 | tf_op jit(solution)/shard_map/moe/pallas_call | solution.py:318
  122.4 1.9 %results.1 = (bf16[128,256]{1,0:T(8,128)(2,1)}, bf16[128,256]{1,0:T(8,128)(2,1)}, f32[1,128,256]{2,1,0:T(8,128)}, f32[1,128,256]{2,1,0:T(8,128)}, f32[1,256,128]{2,1,0:T(8,128)}) custom-call(bf16[128,256]{1,0:T(8,128)(2,1)} %get-tuple-element.10.refs_0_, bf16[128,256]{1,0:T(8,128)(2,1)} %get-tuple-element.11.refs_1_, ...), custom_call_target="tpu_custom_call" | custom-call | tf_op jit(solution)/shard_map/results/pallas_call | solution.py:351
